TPU v7x, 32 devices: a whole 2x2x4 slice. The times are simulated.
32 devices in a mesh: ctx: 16 (over z, y, core), tp: 2 (over x).
Axes of the slice: x: 2, y: 2, z: 4, core: 2. Of those that a mesh axis runs over, the one named last changes fastest.
Arguments:
- tokens: bfloat16 [16384, 1024], P('ctx', 'tp'), may hold values from -6 to 6
- view_counts: int32 [4], replicated, may hold values from 1 to 9, 16 in all
- ln_gain: float32 [1024], replicated, may hold values from 0.25 to 1.75
- w_qkv: bfloat16 [3, 1024, 1024], P(None, None, 'tp'), may hold values from -0.1875 to 0.1875
- head_temp: float32 [16], P('tp'), may hold values from 0.5 to 64
- o_gain: float32 [1024], P('tp'), may hold values from 0.1 to 1.9
- w_o: bfloat16 [1024, 1024], P('tp'), may hold values from -0.25 to 0.25
Outputs:
- mixed: bfloat16 [16384, 1024], P('ctx', 'tp')
Inputs may be any that keep to these rules, and one draw needn't show every extreme that they name: `view_counts`: the view counts sum to 16; the largest is exactly 9.
All inputs are finite; a program needn't handle non-finite values.
Results may differ from a plain program's by a relative error of at most 0.01.
The roundings to bfloat16 on the way count: a program that leaves them out, or rounds other values in their place, can miss the bound.
Values may be sent and summed in bfloat16 or wider, within the bound.
A program may use at most 1 GiB of HBM per device.

v0:
```python
import math

import jax
import jax.numpy as jnp
from jax import lax
from jax.sharding import PartitionSpec as P


def body(tokens, view_counts, ln_gain, w_qkv, head_temp, o_gain, w_o):
    whole = lax.all_gather(tokens, "tp", axis=1, tiled=True)
    xfull = whole.astype(jnp.float32)
    center = xfull - jnp.mean(xfull, axis=-1, keepdims=True)
    spread = jnp.mean(center * center, axis=-1, keepdims=True)
    normed = (center * lax.rsqrt(spread + 1e-05) * ln_gain).astype(jnp.bfloat16)
    proj = jnp.einsum("td,cde->cte", normed, w_qkv, preferred_element_type=jnp.float32).astype(
        jnp.bfloat16
    )
    heads_here = head_temp.shape[0]
    width = proj.shape[2]
    head_size = width // heads_here
    view_tok = tokens.shape[0]
    ends = jnp.cumsum(view_counts)

    def scene_of(views):
        return jnp.sum((ends[None, :] <= views[:, None]).astype(jnp.int32), axis=1)

    own_view = jnp.reshape(lax.axis_index("ctx"), (1,))
    own_scene = scene_of(own_view)[0]
    scale = head_temp / math.sqrt(head_size)
    query3 = proj[0].reshape(view_tok, heads_here, head_size)
    keys2 = lax.all_gather(proj[1], "ctx", axis=0, tiled=True)
    values2 = lax.all_gather(proj[2], "ctx", axis=0, tiled=True)
    rows = keys2.shape[0]
    views = jnp.arange(rows, dtype=jnp.int32) // view_tok
    allowed = scene_of(views) == own_scene
    old_top = jnp.full((heads_here, view_tok), -1e30, jnp.float32)
    keys3 = keys2.reshape(rows, heads_here, head_size)
    values3 = values2.reshape(rows, heads_here, head_size)
    score = jnp.einsum("qhd,khd->hqk", query3, keys3, preferred_element_type=jnp.float32)
    score = jnp.where(allowed[None, None, :], score * scale[:, None, None], -1e30)
    new_top = jnp.maximum(old_top, jnp.max(score, axis=-1))
    weight = jnp.where(allowed[None, None, :], jnp.exp(score - new_top[:, :, None]), 0.0)
    new_total = jnp.sum(weight, axis=-1)
    new_acc = jnp.einsum(
        "hqk,khd->hqd", weight.astype(jnp.bfloat16), values3, preferred_element_type=jnp.float32
    )
    attended = new_acc / new_total[:, :, None]
    level = jnp.mean(attended * attended, axis=-1, keepdims=True)
    gains = o_gain.reshape(heads_here, 1, head_size)
    scaled = attended * lax.rsqrt(level + 1e-05) * gains
    heads_out = jnp.transpose(scaled, (1, 0, 2)).reshape(view_tok, width).astype(jnp.bfloat16)
    terms = jnp.dot(heads_out, w_o, preferred_element_type=jnp.float32)
    summed = lax.psum_scatter(
        terms.astype(jnp.bfloat16), "tp", scatter_dimension=1, tiled=True
    ).astype(jnp.float32)
    return (summed + tokens.astype(jnp.float32)).astype(jnp.bfloat16)


def solution(mesh):
    in_specs = (P("ctx", "tp"), P(), P(), P(None, None, "tp"), P("tp"), P("tp"), P("tp", None))
    out_specs = P("ctx", "tp")
    return jax.shard_map(body, mesh=mesh, in_specs=in_specs, out_specs=out_specs, check_vma=False)
```

profile of v0, /device:TPU:16, one launch (start us, length us, event | category | flops | bytes accessed | tf_op | source)
XLA Modules:
  0.0 755.0 jit_solution(7420514354144506331)
XLA Ops:
  6.5 0.0 copy-start
  6.5 0.0 copy-start.4
  6.5 0.0 all-gather.6.cloned.1.call-start
  6.5 0.7 all-gather.6.cloned.1.call-update
  7.3 0.0 all-gather.8.cloned.1.call-start
  7.3 35.8 %all-gather.6.cloned.1.call-done = bf16[1024,1024]{1,0:T(8,128)(2,1)} async-done(((bf16[1024,512]{1,0:T(8,128)(2,1)}), bf16[1024,1024]{1,0:T(8,128)(2,1)}) %all-gather.6.cloned.1.call-update) | async-done | bytes 2097168 | tf_op jit(solution)/shard_map/all_gather | solution.py:10
  43.1 0.0 copy-start.1
  43.1 2.1 convert_reduce_fusion
  45.2 2.3 fusion.7
  47.5 0.0 copy-done
  47.5 0.0 copy-done.4
  47.5 0.0 copy-done.1
  47.5 4.3 convert_bitcast_fusion
  51.8 0.0 copy-start.3
  51.8 0.0 copy-start.5
  51.9 0.0 copy-start.6
  51.9 1.8 fusion.24
  53.6 0.0 all-gather.8.cloned.1.call-update
  53.7 0.0 all-gather.10.cloned.1.call-start
  53.7 0.0 copy-done.3
  53.7 0.7 mul.60
  54.4 0.0 copy-done.5
  54.4 0.2 reduce-window.4
  54.6 0.7 fusion.21
  55.3 0.2 convert_reduce_fusion.1
  55.5 0.0 copy-done.6
  55.6 0.7 broadcast_compare_fusion
  56.3 0.0 all-gather.10.cloned.1.call-update
  56.3 0.2 reduce-scatter.2.cloned.1.call-start
  56.5 123.3 %all-gather.8.cloned.1.call-done = bf16[1,16384,512]{1,2,0:T(8,128)(2,1)} async-done(((bf16[1,1024,512]{1,2,0:T(8,128)(2,1)}), bf16[1,16384,512]{1,2,0:T(8,128)(2,1)}) %all-gather.8.cloned.1.call-update) | async-done | bytes 16777232 | tf_op jit(solution)/shard_map/all_gather | solution.py:31
  179.8 187.0 %fusion = (f32[8,1024]{1,0:T(8,128)S(1)}, f32[8,1024,16384]{2,1,0:T(8,128)}) fusion(f32[8]{0:T(128)S(1)} %broadcast_multiply_fusion.1, pred[16384]{0:T(1024)(128)(4,1)S(1)} %broadcast_compare_fusion, bf16[1024,8,64]{0,2,1:T(8,128)(2,1)} %bitcast.29, bf16[16384,8,64]{0,2,1:T(8,128)(2,1)} %bitcast.28), kind=kOutput, calls=%fused_computation.2 | convolution fusion | flops 17582514176 | bytes 554745856 | tf_op jit(solution)/shard_map/qhd,khd->hqk/dot_general | solution.py:39
  366.8 171.1 %fusion.1 = f32[8,1024]{1,0:T(8,128)S(1)} fusion(f32[8,1024,16384]{2,1,0:T(8,128)} %get-tuple-element.9, f32[8,1024]{1,0:T(8,128)S(1)} %broadcast_maximum_fusion, f32[8]{0:T(128)S(1)} %broadcast_multiply_fusion.1, pred[16384]{0:T(1024)(128)(4,1)S(1)} %broadcast_compare_fusion), kind=kLoop, calls=%fused_computation.3 | loop fusion | flops 671080448 | bytes 536952832 | tf_op jit(solution)/shard_map/reduce_sum | solution.py:43
  537.9 0.0 all-gather.10.cloned.1.call-done
  537.9 0.0 copy-start.2
  537.9 170.7 %multiply_reduce_fusion = (f32[8,1024]{1,0:T(8,128)S(1)}, f32[8,1024,64]{1,2,0:T(8,128)}) fusion(f32[8,1024]{1,0:T(8,128)S(1)} %fusion.1, bf16[16384,8,64]{0,2,1:T(8,128)(2,1)} %bitcast.33, f32[8,1024,16384]{2,1,0:T(8,128)} %get-tuple-element.9, f32[8,1024]{1,0:T(8,128)S(1)} %broadcast_maximum_fusion, f32[8]{0:T(128)S(1)} %broadcast_multiply_fusion.1, ...), kind=kOutput, calls=%fused_computation.20 | convolution fusion | flops 17852522496 | bytes 555859968 | tf_op jit(solution)/shard_map/hqk,khd->hqd/dot_general | solution.py:44
  708.7 0.0 copy-done.2
  708.7 2.0 fusion.14
  710.7 3.9 convolution_convert_fusion
  714.6 0.0 reduce-scatter.2.cloned.1.call-update
  714.6 31.1 %reduce-scatter.2.cloned.1.call-done = bf16[1024,512]{1,0:T(8,128)(2,1)} async-done(((bf16[1024,1024]{1,0:T(8,128)(2,1)}), bf16[1024,512]{1,0:T(8,128)(2,1)}) %reduce-scatter.2.cloned.1.call-update) | async-done | bytes 1048592 | tf_op jit(solution)/shard_map/reduce_scatter | solution.py:53
  745.7 2.8 add_convert_fusion
  (6 shorter events, 0.0 us)
Async XLA Ops:
  6.5 41.0 %copy-start = (bf16[3,1024,512]{2,1,0:T(8,128)(2,1)S(1)}, bf16[3,1024,512]{2,1,0:T(8,128)(2,1)}, u32[]{:S(2)}) copy-start(bf16[3,1024,512]{2,1,0:T(8,128)(2,1)} %param.10) | copy-start | bytes 9437188
  6.5 41.0 %copy-start.4 = (f32[1024]{0:T(1024)S(1)}, f32[1024]{0:T(1024)}, u32[]{:S(2)}) copy-start(f32[1024]{0:T(1024)} %param.9) | copy-start | bytes 12292
  6.5 36.6 %all-gather.6.cloned.1.call-start = ((), (), s32[]{:S(2)}) async-start(), calls=%async_computation.1 | async-start | bytes 3145728 | tf_op jit(solution)/shard_map/all_gather | solution.py:10
  7.3 172.6 %all-gather.8.cloned.1.call-start = ((), (), s32[]{:S(2)}) async-start(), calls=%async_computation.3 | async-start | bytes 17825792 | tf_op jit(solution)/shard_map/all_gather | solution.py:31
  43.1 4.4 copy-start.1
  51.8 1.9 copy-start.3
  51.8 2.5 copy-start.5
  51.9 3.7 copy-start.6
  53.7 484.2 %all-gather.10.cloned.1.call-start = ((), (), s32[]{:S(2)}) async-start(), calls=%async_computation.4 | async-start | bytes 17825792 | tf_op jit(solution)/shard_map/all_gather | solution.py:32
  56.3 689.4 %reduce-scatter.2.cloned.1.call-start = ((), (), s32[]{:S(2)}) async-start(), calls=%async_computation.2 | async-start | bytes 3145728 | tf_op jit(solution)/shard_map/reduce_scatter | solution.py:53
  537.9 170.8 %copy-start.2 = (f32[8,64]{1,0:T(8,128)S(1)}, f32[8,64]{1,0:T(8,128)}, u32[]{:S(2)}) copy-start(f32[8,64]{1,0:T(8,128)} %mul.60) | copy-start | bytes 6148
Sparse Core Ops, SparseCore 0:
  8.9 34.1 all-gather.5
  53.8 125.9 all-gather.7
  182.0 125.0 all-gather.9
  714.7 30.9 reduce-scatter.1
where the time goes:
time: 757 us; the launch traced here: 755 us
  matrix products  366 us (48%)
  waiting for transfers between devices  191 us (25%)
  other arithmetic  182 us (24%)
  between operations  13.3 us (2%)
    dot_general x1, matrix products, body(): jnp.einsum('qhd,khd->hqk', query3, keys3, preferred_element_type=jnp.floa...  187 us
    reduce_sum x1, other arithmetic, body(): new_total = jnp.sum(weight, axis=-1)  171 us
    dot_general x1, matrix products, body(): jnp.einsum('hqk,khd->hqd', weight.astype(jnp.bfloat16), values3, preferre...  171 us
    all_gather x1, waiting for transfers between devices, body(): keys2 = lax.all_gather(proj[1], 'ctx', axis=0, tiled=True)  123 us
    all_gather x1, waiting for transfers between devices, body(): whole = lax.all_gather(tokens, 'tp', axis=1, tiled=True)  35.8 us
    reduce_scatter x1, waiting for transfers between devices, body(): lax.psum_scatter(terms.astype(jnp.bfloat16), 'tp', scatter_dimension=1, t...  31.1 us
  transfers between devices with their start and end apart: 4, of which 3 were waited for; matrix products, arithmetic and copies ran while one was open for 48% of the time, Pallas kernels for 0%

commit v1 on v0

v1 whole, which is shorter than its diff:
```python
import functools
import math

import jax
import jax.numpy as jnp
from jax import lax
from jax.experimental import pallas as pl
from jax.experimental.pallas import tpu as pltpu
from jax.sharding import PartitionSpec as P

BF16 = jnp.bfloat16
F32 = jnp.float32
LOG2E = 1.4426950408889634
LANES = 128
ROW_TILE = 256


def attention_kernel(hs, span, c_ref, q_ref, k_ref, v_ref, g_ref, o_ref, q_s, top_s, acc_s):
    j = pl.program_id(0)
    rows, width = q_ref.shape
    per = width // hs
    tile = min(ROW_TILE, rows)
    lane = lax.broadcasted_iota(jnp.int32, (rows, width), 1) // hs

    @pl.when(j == 0)
    def _():
        for h in range(per):
            q_s[h] = jnp.where(lane == h, q_ref[...], jnp.zeros((), BF16))
        top_s[...] = jnp.full_like(top_s, -1e30)
        acc_s[...] = jnp.zeros_like(acc_s)

    @pl.when(j < span[1])
    def _():
        keys = k_ref[...]
        values = [jnp.where(lane == h, v_ref[...], jnp.ones((), BF16)) for h in range(per)]
        steps = [(h, i) for i in range(rows // tile) for h in range(per)]

        def score(h, i):
            return lax.dot_general(
                q_s[h, pl.ds(i * tile, tile), :],
                keys,
                (((1,), (1,)), ((), ())),
                preferred_element_type=F32,
            )

        after = score(*steps[0])
        for n, (h, i) in enumerate(steps):
            s = after
            if n + 1 < len(steps):
                after = score(*steps[n + 1])
            at = pl.ds(i * tile, tile)
            old = top_s[h, at, :]
            new = jnp.maximum(old, jnp.max(s, axis=1, keepdims=True))
            top_s[h, at, :] = new
            shrink = jnp.exp2((old - new) * c_ref[h])
            p = jnp.exp2((s - new[:, :1]) * c_ref[h]).astype(BF16)
            term = jnp.dot(p, values[h], preferred_element_type=F32)
            acc_s[h, at, :] = acc_s[h, at, :] * shrink + term

    @pl.when(j == pl.num_programs(0) - 1)
    def _():
        out = jnp.zeros((rows, width), F32)
        for h in range(per):
            acc = acc_s[h]
            total = acc[:, ((h + 1) % per) * hs : ((h + 1) % per) * hs + 1]
            attended = jnp.where(lane == h, acc / total, 0.0)
            level = jnp.sum(attended * attended, axis=1, keepdims=True) / hs
            out = out + attended * lax.rsqrt(level + 1e-05)
        o_ref[...] = (out * g_ref[...]).astype(BF16)


def attention(span, c, query, kv, gain, hs, busy):
    rows, width = query.shape
    views = kv.shape[0] // rows
    per = width // hs

    def view(j, s):
        return s[0] + jnp.minimum(j, s[1] - 1)

    return pl.pallas_call(
        functools.partial(attention_kernel, hs),
        out_shape=jax.ShapeDtypeStruct((rows, width), BF16),
        grid_spec=pltpu.PrefetchScalarGridSpec(
            num_scalar_prefetch=1,
            grid=(views,),
            in_specs=[
                pl.BlockSpec(memory_space=pltpu.SMEM),
                pl.BlockSpec((rows, width), lambda j, s: (0, 0)),
                pl.BlockSpec((rows, width), lambda j, s: (view(j, s), 0)),
                pl.BlockSpec((rows, width), lambda j, s: (view(j, s), 1)),
                pl.BlockSpec((1, width), lambda j, s: (0, 0)),
            ],
            out_specs=pl.BlockSpec((rows, width), lambda j, s: (0, 0)),
            scratch_shapes=[
                pltpu.VMEM((per, rows, width), BF16),
                pltpu.VMEM((per, rows, LANES), F32),
                pltpu.VMEM((per, rows, width), F32),
            ],
        ),
        compiler_params=pltpu.CompilerParams(vmem_limit_bytes=48 << 20),
        cost_estimate=pl.CostEstimate(
            flops=8 * rows * rows * busy * width * per,
            bytes_accessed=4 * rows * busy * width,
            transcendentals=rows * rows * busy * per,
        ),
    )(span, c, query, kv, kv, gain)


def body(tp, tokens, view_counts, ln_gain, w_qkv, head_temp, o_gain, w_o):
    rows, part = tokens.shape
    me = lax.axis_index("tp")
    swap = [(0, 1), (1, 0)]
    if tp == 2:
        other = lax.ppermute(tokens, "tp", swap)
        whole = jnp.where(
            me == 0,
            jnp.concatenate([tokens, other], axis=1),
            jnp.concatenate([other, tokens], axis=1),
        )
    else:
        whole = lax.all_gather(tokens, "tp", axis=1, tiled=True)
    xfull = whole.astype(F32)
    center = xfull - jnp.mean(xfull, axis=-1, keepdims=True)
    spread = jnp.mean(center * center, axis=-1, keepdims=True)
    normed = (center * lax.rsqrt(spread + 1e-05) * ln_gain).astype(BF16)

    heads_here = head_temp.shape[0]
    width = w_qkv.shape[2]
    hs = width // heads_here
    per = LANES // hs
    chunks = width // LANES
    ends = jnp.cumsum(view_counts)
    own_view = lax.axis_index("ctx")
    own_scene = jnp.sum((ends <= own_view).astype(jnp.int32))
    count = view_counts[own_scene]
    span = jnp.stack([ends[own_scene] - count, count]).astype(jnp.int32)
    c = head_temp * (LOG2E / math.sqrt(hs))

    def cut(array, i):
        return lax.slice_in_dim(array, i * LANES, (i + 1) * LANES, axis=-1)

    queries, gathered = [], []
    for i in range(chunks):
        w_kv = jnp.concatenate([cut(w_qkv[1], i), cut(w_qkv[2], i)], axis=1)
        kv = jnp.dot(normed, w_kv, preferred_element_type=F32).astype(BF16)
        if gathered:
            kv, gathered[-1] = lax.optimization_barrier((kv, gathered[-1]))
        gathered.append(lax.all_gather(kv, "ctx", axis=0, tiled=True))
    query = jnp.dot(normed, w_qkv[0], preferred_element_type=F32).astype(BF16)
    queries = [cut(query, i) for i in range(chunks)]
    views = lax.axis_size("ctx")

    if tp == 2:
        out_here = lax.dynamic_slice_in_dim(w_o, me * part, part, axis=1)
        out_there = lax.dynamic_slice_in_dim(w_o, (1 - me) * part, part, axis=1)
        out_there, _ = lax.optimization_barrier((out_there, whole))
        out_there = lax.ppermute(out_there, "tp", swap)
    total = tokens.astype(F32)
    outs = []
    for i in range(chunks):
        heads = attention(
            span,
            c[i * per : (i + 1) * per],
            queries[i],
            gathered[i],
            o_gain[i * LANES : (i + 1) * LANES].reshape(1, LANES),
            hs,
            views // 2 + 1,
        )
        if tp == 2:
            at = slice(i * LANES, (i + 1) * LANES)
            received = lax.ppermute(heads, "tp", swap)
            total = total + jnp.dot(heads, out_here[at], preferred_element_type=F32)
            total = total + jnp.dot(received, out_there[at], preferred_element_type=F32)
        else:
            outs.append(heads)
    if tp != 2:
        heads_out = jnp.concatenate(outs, axis=1)
        terms = jnp.dot(heads_out, w_o, preferred_element_type=F32)
        total = total + lax.psum_scatter(
            terms.astype(BF16), "tp", scatter_dimension=1, tiled=True
        ).astype(F32)
    return total.astype(BF16)


def solution(mesh):
    in_specs = (P("ctx", "tp"), P(), P(), P(None, None, "tp"), P("tp"), P("tp"), P("tp", None))
    out_specs = P("ctx", "tp")
    return jax.shard_map(
        functools.partial(body, mesh.shape["tp"]),
        mesh=mesh,
        in_specs=in_specs,
        out_specs=out_specs,
        check_vma=False,
    )
```

time: 757 us -> 435 us (0.57)
  matrix products: 366 us -> 24.6 us
  other arithmetic: 182 us -> 3.8 us
  Pallas kernels: 0 us -> 117 us
  waiting for transfers between devices: 191 us -> 260 us
    dot_general x4 -> x13, matrix products: 366 us -> 24.6 us  [the longest x4 9.12 us: body(): kv = jnp.dot(normed, w_kv, preferred_element_type=F32).astype(BF16)]
    reduce_sum x3 -> x1, other arithmetic: 172 us -> 0.7 us  [body(): own_scene = jnp.sum((ends <= own_view).astype(jnp.int32))]
    pallas_call x0 -> x4, Pallas kernels: none -> 117 us  [attention(): pl.pallas_call(functools.partial(attention_kernel, hs), out_shape=jax.Sha...]
    all_gather x3 -> x4, waiting for transfers between devices: 159 us -> 218 us  [body(): gathered.append(lax.all_gather(kv, 'ctx', axis=0, tiled=True))]
    ppermute x0 -> x6, waiting for transfers between devices: none -> 42.4 us  [the longest x4 21.7 us: body(): received = lax.ppermute(heads, 'tp', swap)]
    reduce_scatter x1 -> x0, waiting for transfers between devices: 31.1 us -> none  [body(): lax.psum_scatter(terms.astype(jnp.bfloat16), 'tp', scatter_dimension=1, t...]
  transfers between devices with their start and end apart: 4 -> 10, of which waited for: 3 -> 8; matrix products, arithmetic and copies ran while one was open for 48% -> 6% of each run, Pallas kernels for 0% -> 20%
where the time goes in v1:
time: 435 us; the launch traced here: 433 us
  waiting for transfers between devices  260 us (60%)
  Pallas kernels  117 us (27%)
  matrix products  24.6 us (6%)
  between operations  16.7 us (4%)
  starting transfers between devices  5.98 us (1%)
  local copies, waits for them, and re-layouts  4.51 us (1%)
    all_gather x4, waiting for transfers between devices, body(): gathered.append(lax.all_gather(kv, 'ctx', axis=0, tiled=True))  218 us
    pallas_call x4, Pallas kernels, attention(): pl.pallas_call(functools.partial(attention_kernel, hs), out_shape=jax.Sha...  117 us
    ppermute x4, waiting for transfers between devices, body(): received = lax.ppermute(heads, 'tp', swap)  21.7 us
    ppermute x1, waiting for transfers between devices, body(): other = lax.ppermute(tokens, 'tp', swap)  20.7 us
    dot_general x4, matrix products, body(): kv = jnp.dot(normed, w_kv, preferred_element_type=F32).astype(BF16)  9.12 us
  transfers between devices with their start and end apart: 10, of which 8 were waited for; matrix products, arithmetic and copies ran while one was open for 6% of the time, Pallas kernels for 20%

profile of v1, /device:TPU:16, one launch (start us, length us, event | category | flops | bytes accessed | tf_op | source)
XLA Modules:
  0.0 433.1 jit_solution(172782740346820807)
XLA Ops:
  6.5 0.0 copy-start
  6.5 0.0 all-gather.5.cloned.1.call-start
  6.5 1.5 collective-permute-start
  8.0 1.7 slice_bitcast_fusion.1
  9.7 0.0 copy-start.6
  9.7 1.3 fusion.41
  11.0 20.7 %collective-permute-done = bf16[1024,512]{1,0:T(8,128)(2,1)S(1)} collective-permute-done((bf16[1024,512]{1,0:T(8,128)(2,1)}, bf16[1024,512]{1,0:T(8,128)(2,1)S(1)}, u32[]{:S(2)}, u32[]{:S(2)}) %collective-permute-start) | collective-permute-done | bytes 1048608 | tf_op jit(solution)/shard_map/ppermute | solution.py:114
  31.6 0.0 copy-done.6
  31.7 0.8 convert_reduce_fusion
  32.4 0.0 copy-start.8
  32.5 0.7 fusion.2
  33.2 0.0 copy-done.8
  33.2 0.7 fusion.4
  33.9 1.5 convolution_convert_fusion.3
  35.4 0.0 all-gather.5.cloned.1.call-update
  35.4 0.0 all-gather.7.cloned.1.call-start
  35.5 2.5 convolution_convert_fusion.4
  38.0 72.7 %all-gather.5.cloned.1.call-done.k_ref.v_ref = bf16[16384,256]{1,0:T(8,128)(2,1)} async-done(((bf16[1024,256]{1,0:T(8,128)(2,1)}), bf16[16384,256]{1,0:T(8,128)(2,1)}) %all-gather.5.cloned.1.call-update) | async-done | bytes 8388624 | tf_op jit(solution)/shard_map/all_gather | solution.py:148
  110.7 0.0 all-gather.7.cloned.1.call-update
  110.7 0.0 all-gather.9.cloned.1.call-start
  110.8 2.6 convolution_convert_fusion.2
  113.4 72.7 %all-gather.7.cloned.1.call-done.k_ref.v_ref = bf16[16384,256]{1,0:T(8,128)(2,1)} async-done(((bf16[1024,256]{1,0:T(8,128)(2,1)}), bf16[16384,256]{1,0:T(8,128)(2,1)}) %all-gather.7.cloned.1.call-update) | async-done | bytes 8388624 | tf_op jit(solution)/shard_map/all_gather | solution.py:148
  186.0 0.0 all-gather.9.cloned.1.call-update
  186.1 0.2 all-gather.11.cloned.1.call-start
  186.3 0.0 copy-start.10
  186.3 0.0 copy-start.11
  186.3 0.0 copy-start.9
  186.3 2.5 convolution_convert_fusion.1
  188.8 72.6 %all-gather.9.cloned.1.call-done.k_ref.v_ref = bf16[16384,256]{1,0:T(8,128)(2,1)} async-done(((bf16[1024,256]{1,0:T(8,128)(2,1)}), bf16[16384,256]{1,0:T(8,128)(2,1)}) %all-gather.9.cloned.1.call-update) | async-done | bytes 8388624 | tf_op jit(solution)/shard_map/all_gather | solution.py:148
  261.4 0.0 all-gather.11.cloned.1.call-update
  261.4 0.0 copy-done.10
  261.4 0.2 reduce-window.4
  261.6 0.7 fusion.35
  264.4 0.7 dynamic_slice.13
  265.0 0.6 constant_dynamic-slice_fusion.1
  266.8 0.8 pad_add_fusion.span
  267.6 0.1 fusion.43
  267.7 0.0 copy-done.9
  267.7 1.5 collective-permute-start.2
  269.2 2.5 convolution_convert_fusion
  271.8 0.2 fusion.40
  272.0 29.2 %shard_map.73 = bf16[1024,128]{1,0:T(8,128)(2,1)S(1)} custom-call(s32[2]{0:T(128)S(1)} %pad_add_fusion.span, f32[2]{0:T(128)S(1)} %get-tuple-element.39.c_ref, bf16[1024,128]{1,0:T(8,128)(2,1)S(1)} %get-tuple-element.23.q_ref, bf16[16384,256]{1,0:T(8,128)(2,1)} %all-gather.5.cloned.1.call-done.k_ref.v_ref, ...), custom_call_target="tpu_custom_call" | custom-call | flops 19327352832 | bytes 4718592 | tf_op jit(solution)/shard_map/pallas_call | solution.py:80
  301.1 0.6 collective-permute-start.1
  301.8 0.4 fusion.32
  302.2 0.0 collective-permute-done.2
  302.2 7.2 %collective-permute-done.1 = bf16[1024,128]{1,0:T(8,128)(2,1)S(1)} collective-permute-done((bf16[1024,128]{1,0:T(8,128)(2,1)S(1)}, bf16[1024,128]{1,0:T(8,128)(2,1)S(1)}, u32[]{:S(2)}, u32[]{:S(2)}) %collective-permute-start.1) | collective-permute-done | bytes 262176 | tf_op jit(solution)/shard_map/ppermute | solution.py:172
  309.4 1.8 fusion.30
  311.2 29.1 %shard_map.74 = bf16[1024,128]{1,0:T(8,128)(2,1)S(1)} custom-call(s32[2]{0:T(128)S(1)} %pad_add_fusion.span, f32[2]{0:T(128)S(1)} %get-tuple-element.42.c_ref, bf16[1024,128]{1,0:T(8,128)(2,1)S(1)} %get-tuple-element.26.q_ref, bf16[16384,256]{1,0:T(8,128)(2,1)} %all-gather.7.cloned.1.call-done.k_ref.v_ref, ...), custom_call_target="tpu_custom_call" | custom-call | flops 19327352832 | bytes 4718592 | tf_op jit(solution)/shard_map/pallas_call | solution.py:80
  340.3 0.6 collective-permute-start.3
  341.0 1.8 fusion.28
  342.8 5.1 %collective-permute-done.3 = bf16[1024,128]{1,0:T(8,128)(2,1)S(1)} collective-permute-done((bf16[1024,128]{1,0:T(8,128)(2,1)S(1)}, bf16[1024,128]{1,0:T(8,128)(2,1)S(1)}, u32[]{:S(2)}, u32[]{:S(2)}) %collective-permute-start.3) | collective-permute-done | bytes 262176 | tf_op jit(solution)/shard_map/ppermute | solution.py:172
  347.8 1.8 fusion.26
  349.6 29.4 %shard_map.75 = bf16[1024,128]{1,0:T(8,128)(2,1)S(1)} custom-call(s32[2]{0:T(128)S(1)} %pad_add_fusion.span, f32[2]{0:T(128)S(1)} %get-tuple-element.41.c_ref, bf16[1024,128]{1,0:T(8,128)(2,1)S(1)} %get-tuple-element.25.q_ref, bf16[16384,256]{1,0:T(8,128)(2,1)} %all-gather.9.cloned.1.call-done.k_ref.v_ref, ...), custom_call_target="tpu_custom_call" | custom-call | flops 19327352832 | bytes 4718592 | tf_op jit(solution)/shard_map/pallas_call | solution.py:80
  379.0 0.7 collective-permute-start.4
  379.7 1.8 fusion.24
  381.4 4.1 collective-permute-done.4
  385.6 1.8 fusion.22
  387.4 0.0 copy-start.5
  387.4 29.4 %shard_map.76 = bf16[1024,128]{1,0:T(8,128)(2,1)S(1)} custom-call(s32[2]{0:T(128)S(1)} %pad_add_fusion.span, f32[2]{0:T(128)S(1)} %get-tuple-element.40.c_ref, bf16[1024,128]{1,0:T(8,128)(2,1)S(1)} %get-tuple-element.24.q_ref, bf16[16384,256]{1,0:T(8,128)(2,1)} %all-gather.11.cloned.1.call-done.k_ref.v_ref, ...), custom_call_target="tpu_custom_call" | custom-call | flops 19327352832 | bytes 4718592 | tf_op jit(solution)/shard_map/pallas_call | solution.py:80
  416.8 0.7 collective-permute-start.5
  417.6 0.4 fusion.20
  418.0 5.3 %collective-permute-done.5 = bf16[1024,128]{1,0:T(8,128)(2,1)S(1)} collective-permute-done((bf16[1024,128]{1,0:T(8,128)(2,1)S(1)}, bf16[1024,128]{1,0:T(8,128)(2,1)S(1)}, u32[]{:S(2)}, u32[]{:S(2)}) %collective-permute-start.5) | collective-permute-done | bytes 262176 | tf_op jit(solution)/shard_map/ppermute | solution.py:172
  423.3 0.0 copy-done.2
  423.3 3.3 add_convert_fusion
  (18 shorter events, 0.1 us)
Async XLA Ops:
  6.5 261.1 %copy-start = (bf16[512,1024]{1,0:T(8,128)(2,1)S(1)}, bf16[512,1024]{1,0:T(8,128)(2,1)}, u32[]{:S(2)}) copy-start(bf16[512,1024]{1,0:T(8,128)(2,1)} %param.13) | copy-start | bytes 3145732
  6.5 104.2 %all-gather.5.cloned.1.call-start = ((), (), s32[]{:S(2)}) async-start(), calls=%async_computation | async-start | bytes 8912896 | tf_op jit(solution)/shard_map/all_gather | solution.py:148
  6.5 25.1 %collective-permute-start = (bf16[1024,512]{1,0:T(8,128)(2,1)}, bf16[1024,512]{1,0:T(8,128)(2,1)S(1)}, u32[]{:S(2)}, u32[]{:S(2)}) collective-permute-start(bf16[1024,512]{1,0:T(8,128)(2,1)} %param.7), channel_id=1, source_target_pairs={{0,1},{1,0},{2,3},{3,2},{4,5},{5,4},{6,7},{7,6},{8,9},{9,8},{10,11... | collective-permute-start | bytes 3145736 | tf_op jit(solution)/shard_map/ppermute | solution.py:114
  9.7 21.9 %copy-start.6 = (bf16[1024,512]{1,0:T(8,128)(2,1)S(1)}, bf16[1024,512]{1,0:T(8,128)(2,1)}, u32[]{:S(2)}) copy-start(bf16[1024,512]{1,0:T(8,128)(2,1)} %param.7) | copy-start | bytes 3145732
  32.4 0.7 copy-start.8
  35.4 150.6 %all-gather.7.cloned.1.call-start = ((), (), s32[]{:S(2)}) async-start(), calls=%async_computation.1 | async-start | bytes 8912896 | tf_op jit(solution)/shard_map/all_gather | solution.py:148
  110.7 150.7 %all-gather.9.cloned.1.call-start = ((), (), s32[]{:S(2)}) async-start(), calls=%async_computation.2 | async-start | bytes 8912896 | tf_op jit(solution)/shard_map/all_gather | solution.py:148
  186.1 201.3 %all-gather.11.cloned.1.call-start = ((), (), s32[]{:S(2)}) async-start(), calls=%async_computation.3 | async-start | bytes 8912896 | tf_op jit(solution)/shard_map/all_gather | solution.py:148
  186.3 75.1 %copy-start.10 = (s32[4]{0:T(128)S(1)}, s32[4]{0:T(128)}, u32[]{:S(2)}) copy-start(s32[4]{0:T(128)} %param.8) | copy-start | bytes 52
  186.3 81.3 %copy-start.11 = (f32[8]{0:T(128)S(1)}, f32[8]{0:T(128)}, u32[]{:S(2)}) copy-start(f32[8]{0:T(128)} %param.11) | copy-start | bytes 100
  186.3 81.4 %copy-start.9 = (f32[512]{0:T(512)S(1)}, f32[512]{0:T(512)}, u32[]{:S(2)}) copy-start(f32[512]{0:T(512)} %param.12) | copy-start | bytes 6148
  267.7 34.4 %collective-permute-start.2 = (bf16[512,512]{1,0:T(8,128)(2,1)S(1)}, bf16[512,512]{1,0:T(8,128)(2,1)S(1)}, u32[]{:S(2)}, u32[]{:S(2)}) collective-permute-start(bf16[512,512]{1,0:T(8,128)(2,1)S(1)} %constant_dynamic-slice_fusion), channel_id=1, source_target_pairs={{0,1},{1,0},{2,3},{3,2},{4,5},{5,4},{6,7},{7,6},{8,9},{9,8},{10,11... | collective-permute-start | bytes 1572872 | tf_op jit(solution)/shard_map/ppermute | solution.py:157
  301.1 8.3 %collective-permute-start.1 = (bf16[1024,128]{1,0:T(8,128)(2,1)S(1)}, bf16[1024,128]{1,0:T(8,128)(2,1)S(1)}, u32[]{:S(2)}, u32[]{:S(2)}) collective-permute-start(bf16[1024,128]{1,0:T(8,128)(2,1)S(1)} %shard_map.73), channel_id=1, source_target_pairs={{0,1},{1,0},{2,3},{3,2},{4,5},{5,4},{6,7},{7,6},{8,9},{9,8},{10,11... | collective-permute-start | bytes 786440 | tf_op jit(solution)/shard_map/ppermute | solution.py:172
  302.2 83.4 %copy-start.7 = (bf16[512,512]{1,0:T(8,128)(2,1)}, bf16[512,512]{1,0:T(8,128)(2,1)S(1)}, u32[]{:S(2)}) copy-start(bf16[512,512]{1,0:T(8,128)(2,1)S(1)} %collective-permute-done.2) | copy-start | bytes 1572868
  340.3 7.5 %collective-permute-start.3 = (bf16[1024,128]{1,0:T(8,128)(2,1)S(1)}, bf16[1024,128]{1,0:T(8,128)(2,1)S(1)}, u32[]{:S(2)}, u32[]{:S(2)}) collective-permute-start(bf16[1024,128]{1,0:T(8,128)(2,1)S(1)} %shard_map.74), channel_id=1, source_target_pairs={{0,1},{1,0},{2,3},{3,2},{4,5},{5,4},{6,7},{7,6},{8,9},{9,8},{10,11... | collective-permute-start | bytes 786440 | tf_op jit(solution)/shard_map/ppermute | solution.py:172
  379.0 6.6 %collective-permute-start.4 = (bf16[1024,128]{1,0:T(8,128)(2,1)S(1)}, bf16[1024,128]{1,0:T(8,128)(2,1)S(1)}, u32[]{:S(2)}, u32[]{:S(2)}) collective-permute-start(bf16[1024,128]{1,0:T(8,128)(2,1)S(1)} %shard_map.75), channel_id=1, source_target_pairs={{0,1},{1,0},{2,3},{3,2},{4,5},{5,4},{6,7},{7,6},{8,9},{9,8},{10,11... | collective-permute-start | bytes 786440 | tf_op jit(solution)/shard_map/ppermute | solution.py:172
  387.4 35.9 %copy-start.2 = (f32[1024,512]{1,0:T(8,128)S(1)}, f32[1024,512]{1,0:T(8,128)}, u32[]{:S(2)}) copy-start(f32[1024,512]{1,0:T(8,128)} %fusion.28) | copy-start | bytes 6291460
  387.4 35.9 %copy-start.3 = (f32[1024,512]{1,0:T(8,128)S(1)}, f32[1024,512]{1,0:T(8,128)}, u32[]{:S(2)}) copy-start(f32[1024,512]{1,0:T(8,128)} %fusion.26) | copy-start | bytes 6291460
  387.4 35.9 %copy-start.4 = (f32[1024,512]{1,0:T(8,128)S(1)}, f32[1024,512]{1,0:T(8,128)}, u32[]{:S(2)}) copy-start(f32[1024,512]{1,0:T(8,128)} %fusion.24) | copy-start | bytes 6291460
  387.4 35.9 %copy-start.5 = (f32[1024,512]{1,0:T(8,128)S(1)}, f32[1024,512]{1,0:T(8,128)}, u32[]{:S(2)}) copy-start(f32[1024,512]{1,0:T(8,128)} %fusion.22) | copy-start | bytes 6291460
  416.8 6.5 %copy-start.1 = (f32[1024,512]{1,0:T(8,128)S(1)}, f32[1024,512]{1,0:T(8,128)}, u32[]{:S(2)}) copy-start(f32[1024,512]{1,0:T(8,128)} %fusion.30) | copy-start | bytes 6291460
  416.8 6.4 %collective-permute-start.5 = (bf16[1024,128]{1,0:T(8,128)(2,1)S(1)}, bf16[1024,128]{1,0:T(8,128)(2,1)S(1)}, u32[]{:S(2)}, u32[]{:S(2)}) collective-permute-start(bf16[1024,128]{1,0:T(8,128)(2,1)S(1)} %shard_map.76), channel_id=1, source_target_pairs={{0,1},{1,0},{2,3},{3,2},{4,5},{5,4},{6,7},{7,6},{8,9},{9,8},{10,11... | collective-permute-start | bytes 786440 | tf_op jit(solution)/shard_map/ppermute | solution.py:172
Sparse Core Ops, SparseCore 0:
  35.5 75.1 all-gather.4
  112.9 73.1 all-gather.6
  188.2 73.1 all-gather.8
  263.4 73.1 all-gather.10

commit v2 on v0

v2 whole, which is shorter than its diff:
```python
import functools
import math

import jax
import jax.numpy as jnp
from jax import lax
from jax.experimental import pallas as pl
from jax.experimental.pallas import tpu as pltpu
from jax.sharding import PartitionSpec as P

BF16 = jnp.bfloat16
F32 = jnp.float32
LOG2E = 1.4426950408889634


def attention_kernel(hs, span, c_ref, g_ref, got_ref, *rest):
    *others, o_ref, s_s, top_s, acc_s = rest
    i = pl.program_id(0)
    tile, lanes = o_ref.shape[1:]
    part = got_ref.shape[1] - tile
    first = lax.broadcasted_iota(jnp.int32, (tile, lanes), 1) < hs
    packed = got_ref[i, part:, :].astype(F32)
    queries = [
        jnp.where(first, x, 0.0).astype(BF16) for x in (packed, pltpu.roll(packed, hs, 1))
    ]
    low, count = span[0, i], span[1, i]

    def pairs(j):
        return jnp.concatenate([got_ref[j, :part, :]] + [ref[j] for ref in others], axis=0)

    def score(query, kv):
        return lax.dot_general(
            query, kv, (((1,), (1,)), ((), ())), preferred_element_type=F32
        )

    top_s[...] = jnp.full_like(top_s, -1e30)
    acc_s[...] = jnp.zeros_like(acc_s)
    s_s[...] = score(queries[0], pairs(low))

    def step(n, carry):
        kv = pairs(low + n)
        key_lanes = lax.broadcasted_iota(jnp.int32, kv.shape, 1) < hs
        values = jnp.where(key_lanes, jnp.ones((), BF16), kv)

        def update(t, s):
            old = top_s[t]
            new = jnp.maximum(old, jnp.max(s, axis=1, keepdims=True))
            top_s[t] = new
            shrink = jnp.exp2((old - new) * c_ref[0])
            p = jnp.exp2((s - new[:, :1]) * c_ref[0]).astype(BF16)
            term = jnp.dot(p, values, preferred_element_type=F32)
            acc_s[t] = acc_s[t] * shrink + term

        s1 = score(queries[1], kv)
        update(0, s_s[...])
        s_s[...] = score(queries[0], pairs(low + jnp.minimum(n + 1, count - 1)))
        update(1, s1)
        return carry

    lax.fori_loop(0, count, step, 0)
    scaled = []
    for t in range(2):
        acc = acc_s[t]
        attended = jnp.where(first, 0.0, acc / acc[:, :1])
        level = jnp.sum(attended * attended, axis=1, keepdims=True) / hs
        scaled.append(attended * lax.rsqrt(level + 1e-05))
    out = jnp.where(first, pltpu.roll(scaled[0], hs, 1), scaled[1])
    o_ref[0] = (out * g_ref[...]).astype(BF16)


def attention(span, c, gain, got, others, tile, hs):
    views, depth, lanes = got.shape
    part = depth - tile
    rows = part * (len(others) + 1)
    whole = lambda i, s: (0, 0, 0)
    work = 2 * tile * views * rows * (views // 2)
    return pl.pallas_call(
        functools.partial(attention_kernel, hs),
        out_shape=jax.ShapeDtypeStruct((views, tile, lanes), BF16),
        grid_spec=pltpu.PrefetchScalarGridSpec(
            num_scalar_prefetch=1,
            grid=(views,),
            in_specs=[
                pl.BlockSpec(memory_space=pltpu.SMEM),
                pl.BlockSpec((1, lanes), lambda i, s: (0, 0)),
                pl.BlockSpec((views, depth, lanes), whole),
            ]
            + [pl.BlockSpec((views, part, lanes), whole) for _ in others],
            out_specs=pl.BlockSpec((1, tile, lanes), lambda i, s: (i, 0, 0)),
            scratch_shapes=[
                pltpu.VMEM((tile, rows), F32),
                pltpu.VMEM((2, tile, lanes), F32),
                pltpu.VMEM((2, tile, lanes), F32),
            ],
        ),
        compiler_params=pltpu.CompilerParams(vmem_limit_bytes=48 << 20),
        cost_estimate=pl.CostEstimate(
            flops=4 * work * lanes, bytes_accessed=8 * views * rows * lanes, transcendentals=work
        ),
    )(span, c, gain, got, *others)


def body(tp, tokens, view_counts, ln_gain, w_qkv, head_temp, o_gain, w_o):
    rows, part = tokens.shape
    me = lax.axis_index("tp")
    swap = [(0, 1), (1, 0)]
    if tp == 2:
        other = lax.ppermute(tokens, "tp", swap)
        whole = jnp.where(
            me == 0,
            jnp.concatenate([tokens, other], axis=1),
            jnp.concatenate([other, tokens], axis=1),
        )
    else:
        whole = lax.all_gather(tokens, "tp", axis=1, tiled=True)
    xfull = whole.astype(F32)
    center = xfull - jnp.mean(xfull, axis=-1, keepdims=True)
    spread = jnp.mean(center * center, axis=-1, keepdims=True)
    normed = (center * lax.rsqrt(spread + 1e-05) * ln_gain).astype(BF16)

    heads_here = head_temp.shape[0]
    width = w_qkv.shape[2]
    hs = width // heads_here
    views = lax.axis_size("ctx")
    split = views // heads_here
    cut = rows // split
    tile = cut // 2
    own_view = lax.axis_index("ctx")
    own_head = own_view // split

    ends = jnp.cumsum(view_counts)
    scene = jnp.sum(
        (ends[None, :] <= jnp.arange(views, dtype=jnp.int32)[:, None]).astype(jnp.int32), axis=1
    )
    counts = view_counts[scene]
    span = jnp.stack([ends[scene] - counts, counts]).astype(jnp.int32)
    c = lax.dynamic_slice_in_dim(head_temp, own_head, 1) * (LOG2E / math.sqrt(hs))
    gain = lax.dynamic_slice_in_dim(o_gain, own_head * hs, hs)
    gain = jnp.concatenate([gain, gain]).reshape(1, 2 * hs)

    depth = w_qkv.shape[1]
    w_kv = jnp.transpose(w_qkv[1:].reshape(2, depth, heads_here, hs), (1, 2, 0, 3))
    kv = jnp.dot(
        normed, w_kv.reshape(depth, 2 * width), preferred_element_type=F32
    ).astype(BF16)
    kv = jnp.transpose(kv.reshape(split, cut, heads_here, 2 * hs), (2, 0, 1, 3))
    query = jnp.dot(normed, w_qkv[0], preferred_element_type=F32).astype(BF16)
    query = jnp.transpose(query.reshape(split, 2, tile, heads_here, hs), (3, 0, 2, 1, 4))
    send = jnp.concatenate(
        [kv.reshape(views, cut, 2 * hs), query.reshape(views, tile, 2 * hs)], axis=1
    )
    got = lax.all_to_all(send, "ctx", split_axis=0, concat_axis=0, tiled=True)
    others = []
    for shift in range(1, split):
        perm = [(v, v // split * split + (v + shift) % split) for v in range(views)]
        others.append(lax.ppermute(got[:, :cut], "ctx", perm))
    if tp == 2:
        out_here = lax.dynamic_slice_in_dim(w_o, me * part, part, axis=1)
        out_there = lax.dynamic_slice_in_dim(w_o, (1 - me) * part, part, axis=1)
        out_there, _ = lax.optimization_barrier((out_there, got))
        out_there = lax.ppermute(out_there, "tp", swap)
    heads = attention(span, c, gain, got, others, tile, hs)
    back = lax.all_to_all(heads, "ctx", split_axis=0, concat_axis=0, tiled=True)
    back = jnp.transpose(back.reshape(heads_here, split, tile, 2, hs), (1, 3, 2, 0, 4))
    back = back.reshape(rows, width)
    total = tokens.astype(F32)
    if tp == 2:
        received = lax.ppermute(back, "tp", swap)
        total = total + jnp.dot(back, out_here, preferred_element_type=F32)
        total = total + jnp.dot(received, out_there, preferred_element_type=F32)
    else:
        terms = jnp.dot(back, w_o, preferred_element_type=F32)
        total = total + lax.psum_scatter(
            terms.astype(BF16), "tp", scatter_dimension=1, tiled=True
        ).astype(F32)
    return total.astype(BF16)


def solution(mesh):
    in_specs = (P("ctx", "tp"), P(), P(), P(None, None, "tp"), P("tp"), P("tp"), P("tp", None))
    out_specs = P("ctx", "tp")
    return jax.shard_map(
        functools.partial(body, mesh.shape["tp"]),
        mesh=mesh,
        in_specs=in_specs,
        out_specs=out_specs,
        check_vma=False,
    )
```

time: 757 us -> 303 us (0.40)
  matrix products: 366 us -> 10.7 us
  other arithmetic: 182 us -> 6.69 us
  waiting for transfers between devices: 191 us -> 50.5 us
  blocking collectives: 0 us -> 106 us
  Pallas kernels: 0 us -> 95.1 us
  local copies, waits for them, and re-layouts: 2.47 us -> 27.1 us
  between operations: 13.3 us -> 0.8 us
    dot_general x4, matrix products: 366 us -> 10.7 us  [the longest x1 4 us: body(): jnp.dot(normed, w_kv.reshape(depth, 2 * width), preferred_element_type=F32)]
    reduce_sum x3 -> x1, other arithmetic: 172 us -> 0.09 us  [body(): jnp.sum((ends[None, :] <= jnp.arange(views, dtype=jnp.int32)[:, None]).as...]
    all_gather x3 -> x0, waiting for transfers between devices: 159 us -> none  [the longest x1 123 us: body(): keys2 = lax.all_gather(proj[1], 'ctx', axis=0, tiled=True)]
    all_to_all x0 -> x2, blocking collectives: none -> 106 us  [the longest x1 76.1 us: body(): got = lax.all_to_all(send, 'ctx', split_axis=0, concat_axis=0, tiled=True)]
    pallas_call x0 -> x1, Pallas kernels: none -> 95.1 us  [attention(): pl.pallas_call(functools.partial(attention_kernel, hs), out_shape=jax.Sha...]
    ppermute x0 -> x4, waiting for transfers between devices: none -> 50.5 us  [the longest x1 32.2 us: body(): out_there = lax.ppermute(out_there, 'tp', swap)]
    reduce_scatter x1 -> x0, waiting for transfers between devices: 31.1 us -> none  [body(): lax.psum_scatter(terms.astype(jnp.bfloat16), 'tp', scatter_dimension=1, t...]
    reshape x0 -> x4, local copies, waits for them, and re-layouts: none -> 7.58 us  [the longest x1 2.77 us: body(): query.reshape(split, 2, tile, heads_here, hs)]
  transfers between devices with their start and end apart: 4 -> 4, of which waited for: 3 -> 3; matrix products, arithmetic and copies ran while one was open for 48% -> 3% of each run, Pallas kernels for 0% -> 0%
where the time goes in v2:
time: 303 us; the launch traced here: 300 us
  blocking collectives  106 us (35%)
  Pallas kernels  95.1 us (31%)
  waiting for transfers between devices  50.5 us (17%)
  local copies, waits for them, and re-layouts  27.1 us (9%)
  matrix products  10.7 us (4%)
  other arithmetic  6.69 us (2%)
  starting transfers between devices  3.58 us (1%)
    pallas_call x1, Pallas kernels, attention(): pl.pallas_call(functools.partial(attention_kernel, hs), out_shape=jax.Sha...  95.1 us
    all_to_all x1, blocking collectives, body(): got = lax.all_to_all(send, 'ctx', split_axis=0, concat_axis=0, tiled=True)  76.1 us
    ppermute x1, waiting for transfers between devices, body(): out_there = lax.ppermute(out_there, 'tp', swap)  32.2 us
    all_to_all x1, blocking collectives, body(): back = lax.all_to_all(heads, 'ctx', split_axis=0, concat_axis=0, tiled=True)  29.8 us
    ppermute x1, waiting for transfers between devices, body(): other = lax.ppermute(tokens, 'tp', swap)  17.6 us
  transfers between devices with their start and end apart: 4, of which 3 were waited for; matrix products, arithmetic and copies ran while one was open for 3% of the time, Pallas kernels for 0%

profile of v2, /device:TPU:16, one launch (start us, length us, event | category | flops | bytes accessed | tf_op | source)
XLA Modules:
  0.0 300.4 jit_solution(3777866403317868454)
XLA Ops:
  0.0 0.0 copy-start
  0.0 0.0 slice-start
  0.0 1.5 collective-permute-start
  1.5 0.4 slice-done
  1.9 2.5 copy.26
  4.4 0.0 copy-start.2
  4.4 3.2 %copy.19 = bf16[1024,8,2,64]{0,3,2,1:T(8,128)(2,1)} copy(bf16[1024,8,2,64]{0,3,1,2:T(8,128)(2,1)} %bitcast.43) | data formatting | bytes 4194304 | tf_op jit(solution)/shard_map/transpose | solution.py:142
  7.6 0.0 copy-start.8
  7.6 0.0 copy-start.7
  7.6 17.6 %collective-permute-done = bf16[1024,512]{1,0:T(8,128)(2,1)} collective-permute-done((bf16[1024,512]{1,0:T(8,128)(2,1)}, bf16[1024,512]{1,0:T(8,128)(2,1)}, u32[]{:S(2)}, u32[]{:S(2)}) %collective-permute-start) | collective-permute-done | bytes 1048608 | tf_op jit(solution)/shard_map/ppermute | solution.py:108
  25.2 0.0 copy-done.2
  25.2 2.1 convert_reduce_fusion
  27.3 2.8 fusion.2
  30.1 0.0 copy-done.8
  30.1 0.0 copy-done.7
  30.1 4.0 %convert_bitcast_fusion = bf16[128,8,8,128]{3,1,2,0:T(8,128)(2,1)S(1)} fusion(bf16[1024,1024]{0,1:T(8,128)(2,1)S(1)} %bitcast.48, f32[1024]{0:T(1024)S(1)} %copy-done.8, f32[1024]{0:T(1024)S(1)} %add_rsqrt_fusion, f32[1024]{0:T(1024)S(1)} %broadcast_multiply_fusion, bf16[1024,512]{1,0:T(8,128)(2,1)} %collective-permute-done, ...), kind=kOutput, calls=%fused_computation.12 | convolution fusion | flops 2163212288 | bytes 6303745 | tf_op jit(solution)/shard_map/dot_general | solution.py:143
  34.1 0.6 copy.27
  34.8 0.0 copy-start.6
  34.8 1.8 copy.20
  36.5 0.9 copy-done.6
  37.4 2.9 convolution_convert_fusion
  40.3 1.3 copy.21
  41.6 0.0 copy-start.5
  41.6 2.8 reshape.94
  44.4 2.4 copy.22
  46.8 2.3 copy.23
  49.1 0.0 copy-done.5
  49.1 1.4 pad_maximum_fusion
  50.5 76.1 %all_to_all.10.got_ref = bf16[16,768,128]{2,1,0:T(8,128)(2,1)S(1)} all-to-all(bf16[16,768,128]{2,1,0:T(8,128)(2,1)S(1)} %pad_maximum_fusion), channel_id=1, replica_groups=mesh['ctx'=16,'tp'=2] {'ctx'}, dimensions={0} | all-to-all | bytes 6291456 | tf_op jit(solution)/shard_map/all_to_all | solution.py:152
  126.6 0.0 copy-start.4
  126.6 1.6 copy-done.4
  128.2 0.0 copy-start.1
  128.2 0.0 copy-start.9
  128.2 1.5 slice.16
  129.7 0.0 collective-permute-start.1
  129.7 0.0 copy-done.1
  129.7 0.2 reduce-window.8
  129.9 0.1 convert_reduce_fusion.1
  130.0 0.7 gather_fusion
  130.7 0.7 gather_fusion.1
  131.3 0.8 dynamic_slice.13
  132.1 0.0 copy-done.9
  132.1 0.6 dynamic_slice.12
  133.3 0.1 maximum_bitcast_fusion.g_ref
  133.4 0.7 collective-permute-done.1.rest_0_
  134.1 95.1 %shard_map.73 = bf16[16,256,128]{2,1,0:T(8,128)(2,1)S(1)} custom-call(s32[2,16]{1,0:T(2,128)S(1)} %pad_add_fusion.span, f32[1]{0:T(128)S(6)} %mul.31.c_ref, f32[1,128]{1,0:T(1,128)S(1)} %maximum_bitcast_fusion.g_ref, bf16[16,768,128]{2,1,0:T(8,128)(2,1)} %copy-done.4, bf16[16,512,128]{2,1,0:T(8,128)(2,1)S(1)} %collective-permute-done.1.rest_0_), custom_call_target="tpu_custom_call" | custom-call | flops 34359738368 | bytes 16777216 | tf_op jit(solution)/shard_map/pallas_call | solution.py:77
  229.2 29.8 %all_to_all.11 = bf16[16,256,128]{2,1,0:T(8,128)(2,1)S(1)} all-to-all(bf16[16,256,128]{2,1,0:T(8,128)(2,1)S(1)} %shard_map.73), channel_id=1, replica_groups=mesh['ctx'=16,'tp'=2] {'ctx'}, dimensions={0} | all-to-all | bytes 2097152 | tf_op jit(solution)/shard_map/all_to_all | solution.py:163
  259.0 0.5 copy.24
  259.5 1.1 copy.25
  260.6 0.8 reshape.97
  261.4 1.6 collective-permute-start.2
  262.9 0.0 copy-done
  262.9 0.8 constant_dynamic-slice_fusion
  263.8 0.0 copy-start.3
  263.8 0.5 collective-permute-start.3
  264.3 0.7 fusion.7
  265.0 32.2 %collective-permute-done.3 = bf16[512,512]{1,0:T(8,128)(2,1)} collective-permute-done((bf16[512,512]{1,0:T(8,128)(2,1)}, bf16[512,512]{1,0:T(8,128)(2,1)}, u32[]{:S(2)}, u32[]{:S(2)}) %collective-permute-start.3) | collective-permute-done | bytes 524320 | tf_op jit(solution)/shard_map/ppermute | solution.py:161
  297.3 0.0 collective-permute-done.2
  297.3 0.0 copy-done.3
  297.3 3.1 %add_convert_fusion = bf16[1024,512]{1,0:T(8,128)(2,1)} fusion(f32[1024,512]{1,0:T(8,128)S(1)} %fusion.7, bf16[1024,512]{1,0:T(8,128)(2,1)S(1)} %copy-done.3, bf16[1024,512]{0,1:T(8,128)(2,1)} %collective-permute-done.2, bf16[512,512]{1,0:T(8,128)(2,1)} %collective-permute-done.3), kind=kOutput, calls=%fused_computation.11 | convolution fusion | flops 538968064 | bytes 5767168 | tf_op jit(solution)/shard_map/dot_general | solution.py:170
  (6 shorter events, 0.0 us)
Async XLA Ops:
  0.0 262.9 %copy-start = (bf16[512,1024]{1,0:T(8,128)(2,1)S(1)}, bf16[512,1024]{1,0:T(8,128)(2,1)}, u32[]{:S(2)}) copy-start(bf16[512,1024]{1,0:T(8,128)(2,1)} %param.13) | copy-start | bytes 3145732
  0.0 1.9 slice-start
  0.0 25.2 %collective-permute-start = (bf16[1024,512]{1,0:T(8,128)(2,1)}, bf16[1024,512]{1,0:T(8,128)(2,1)}, u32[]{:S(2)}, u32[]{:S(2)}) collective-permute-start(bf16[1024,512]{1,0:T(8,128)(2,1)} %param.7), channel_id=1, source_target_pairs={{0,1},{1,0},{2,3},{3,2},{4,5},{5,4},{6,7},{7,6},{8,9},{9,8},{10,11... | collective-permute-start | bytes 3145736 | tf_op jit(solution)/shard_map/ppermute | solution.py:108
  4.4 20.8 %copy-start.2 = (bf16[1024,512]{1,0:T(8,128)(2,1)S(1)}, bf16[1024,512]{1,0:T(8,128)(2,1)}, u32[]{:S(2)}) copy-start(bf16[1024,512]{1,0:T(8,128)(2,1)} %param.7) | copy-start | bytes 3145732
  7.6 22.5 %copy-start.8 = (f32[1024]{0:T(1024)S(1)}, f32[1024]{0:T(1024)}, u32[]{:S(2)}) copy-start(f32[1024]{0:T(1024)} %param.9) | copy-start | bytes 12292
  7.6 22.5 %copy-start.7 = (bf16[1024,8,2,64]{0,3,2,1:T(8,128)(2,1)S(1)}, bf16[1024,8,2,64]{0,3,2,1:T(8,128)(2,1)}, u32[]{:S(2)}) copy-start(bf16[1024,8,2,64]{0,3,2,1:T(8,128)(2,1)} %copy.19) | copy-start | bytes 6291460
  34.8 2.7 copy-start.6
  41.6 7.4 %copy-start.5 = (bf16[2,512,8,128]{3,1,0,2:T(8,128)(2,1)S(1)}, bf16[2,512,8,128]{3,1,0,2:T(8,128)(2,1)}, u32[]{:S(2)}) copy-start(bf16[2,512,8,128]{3,1,0,2:T(8,128)(2,1)} %copy.20) | copy-start | bytes 6291460
  126.6 1.6 copy-start.4
  128.2 1.5 copy-start.1
  128.2 3.9 %copy-start.9 = (f32[8]{0:T(128)S(1)}, f32[8]{0:T(128)}, u32[]{:S(2)}) copy-start(f32[8]{0:T(128)} %param.11) | copy-start | bytes 100
  129.7 4.4 %collective-permute-start.1 = (bf16[16,512,128]{2,1,0:T(8,128)(2,1)}, bf16[16,512,128]{2,1,0:T(8,128)(2,1)S(1)}, u32[]{:S(2)}, u32[]{:S(2)}) collective-permute-start(bf16[16,512,128]{2,1,0:T(8,128)(2,1)} %slice.16), channel_id=1, source_target_pairs={{0,2},{2,0},{4,6},{6,4},{8,10},{10,8},{12,14},{14,12},{16,18},{18,... | collective-permute-start | bytes 6291464 | tf_op jit(solution)/shard_map/ppermute | solution.py:156
  261.4 35.9 %collective-permute-start.2 = (bf16[1024,512]{0,1:T(8,128)(2,1)S(1)}, bf16[1024,512]{0,1:T(8,128)(2,1)}, u32[]{:S(2)}, u32[]{:S(2)}) collective-permute-start(bf16[1024,512]{0,1:T(8,128)(2,1)S(1)} %reshape.97), channel_id=1, source_target_pairs={{0,1},{1,0},{2,3},{3,2},{4,5},{5,4},{6,7},{7,6},{8,9},{9,8},{10,11... | collective-permute-start | bytes 3145736 | tf_op jit(solution)/shard_map/ppermute | solution.py:168
  263.8 33.5 %copy-start.3 = (bf16[1024,512]{1,0:T(8,128)(2,1)S(1)}, bf16[1024,512]{1,0:T(8,128)(2,1)}, u32[]{:S(2)}) copy-start(bf16[1024,512]{1,0:T(8,128)(2,1)} %param.7) | copy-start | bytes 3145732
  263.8 33.5 %collective-permute-start.3 = (bf16[512,512]{1,0:T(8,128)(2,1)}, bf16[512,512]{1,0:T(8,128)(2,1)}, u32[]{:S(2)}, u32[]{:S(2)}) collective-permute-start(bf16[512,512]{1,0:T(8,128)(2,1)} %constant_dynamic-slice_fusion), channel_id=1, source_target_pairs={{0,1},{1,0},{2,3},{3,2},{4,5},{5,4},{6,7},{7,6},{8,9},{9,8},{10,11... | collective-permute-start | bytes 1572872 | tf_op jit(solution)/shard_map/ppermute | solution.py:161

commit v3 on v2

--- a/solution.py
+++ b/solution.py
@@ -113,6 +113,11 @@
         )
     else:
         whole = lax.all_gather(tokens, "tp", axis=1, tiled=True)
+    if tp == 2:
+        out_here = lax.dynamic_slice_in_dim(w_o, me * part, part, axis=1)
+        out_there = lax.dynamic_slice_in_dim(w_o, (1 - me) * part, part, axis=1)
+        out_there, whole = lax.optimization_barrier((out_there, whole))
+        out_there = lax.ppermute(out_there, "tp", swap)
     xfull = whole.astype(F32)
     center = xfull - jnp.mean(xfull, axis=-1, keepdims=True)
     spread = jnp.mean(center * center, axis=-1, keepdims=True)
@@ -150,15 +155,12 @@
         [kv.reshape(views, cut, 2 * hs), query.reshape(views, tile, 2 * hs)], axis=1
     )
     got = lax.all_to_all(send, "ctx", split_axis=0, concat_axis=0, tiled=True)
+    if tp == 2:
+        got, out_there = lax.optimization_barrier((got, out_there))
     others = []
     for shift in range(1, split):
         perm = [(v, v // split * split + (v + shift) % split) for v in range(views)]
         others.append(lax.ppermute(got[:, :cut], "ctx", perm))
-    if tp == 2:
-        out_here = lax.dynamic_slice_in_dim(w_o, me * part, part, axis=1)
-        out_there = lax.dynamic_slice_in_dim(w_o, (1 - me) * part, part, axis=1)
-        out_there, _ = lax.optimization_barrier((out_there, got))
-        out_there = lax.ppermute(out_there, "tp", swap)
     heads = attention(span, c, gain, got, others, tile, hs)
     back = lax.all_to_all(heads, "ctx", split_axis=0, concat_axis=0, tiled=True)
     back = jnp.transpose(back.reshape(heads_here, split, tile, 2, hs), (1, 3, 2, 0, 4))

time: 303 us -> 293 us (0.967)
  blocking collectives: 106 us -> 29.6 us
  waiting for transfers between devices: 50.5 us -> 107 us
  starting transfers between devices: 3.58 us -> 10.9 us
  Pallas kernels: 95.1 us -> 98.4 us
    all_to_all x1 -> x0, blocking collectives: 76.1 us -> none  [body(): got = lax.all_to_all(send, 'ctx', split_axis=0, concat_axis=0, tiled=True)]
    all_to_all x0 -> x1, waiting for transfers between devices: none -> 56.1 us  [body(): got = lax.all_to_all(send, 'ctx', split_axis=0, concat_axis=0, tiled=True)]
    ppermute x1, waiting for transfers between devices: 0.01 us -> 22.3 us  [body(): received = lax.ppermute(back, 'tp', swap)]
    ppermute x1, waiting for transfers between devices: 32.2 us -> 12.5 us  [body(): out_there = lax.ppermute(out_there, 'tp', swap)]
    all_to_all x0 -> x1, starting transfers between devices: none -> 6.32 us  [body(): got = lax.all_to_all(send, 'ctx', split_axis=0, concat_axis=0, tiled=True)]
    pallas_call x1, Pallas kernels: 95.1 us -> 98.4 us  [attention(): pl.pallas_call(functools.partial(attention_kernel, hs), out_shape=jax.Sha...]
    select_n x0 -> x1, other arithmetic: none -> 3.03 us  [body(): jnp.where(me == 0, jnp.concatenate([tokens, other], axis=1), jnp.concaten...]
  transfers between devices with their start and end apart: 4 -> 5, of which waited for: 3 -> 5; matrix products, arithmetic and copies ran while one was open for 3% -> 4% of each run, Pallas kernels for 0% -> 0%
where the time goes in v3:
time: 293 us; the launch traced here: 292 us
  waiting for transfers between devices  107 us (37%)
  Pallas kernels  98.4 us (34%)
  blocking collectives  29.6 us (10%)
  local copies, waits for them, and re-layouts  29.2 us (10%)
  starting transfers between devices  10.9 us (4%)
  matrix products  8.56 us (3%)
  other arithmetic  7.6 us (3%)
    pallas_call x1, Pallas kernels, attention(): pl.pallas_call(functools.partial(attention_kernel, hs), out_shape=jax.Sha...  98.4 us
    all_to_all x1, waiting for transfers between devices, body(): got = lax.all_to_all(send, 'ctx', split_axis=0, concat_axis=0, tiled=True)  56.1 us
    all_to_all x1, blocking collectives, body(): back = lax.all_to_all(heads, 'ctx', split_axis=0, concat_axis=0, tiled=True)  29.6 us
    ppermute x1, waiting for transfers between devices, body(): received = lax.ppermute(back, 'tp', swap)  22.3 us
    ppermute x1, waiting for transfers between devices, body(): other = lax.ppermute(tokens, 'tp', swap)  15.2 us
    ppermute x1, waiting for transfers between devices, body(): out_there = lax.ppermute(out_there, 'tp', swap)  12.5 us
    all_to_all x1, starting transfers between devices, body(): got = lax.all_to_all(send, 'ctx', split_axis=0, concat_axis=0, tiled=True)  6.32 us
  transfers between devices with their start and end apart: 5, of which 5 were waited for; matrix products, arithmetic and copies ran while one was open for 4% of the time, Pallas kernels for 0%

profile of v3, /device:TPU:16, one launch (start us, length us, event | category | flops | bytes accessed | tf_op | source)
XLA Modules:
  0.0 291.9 jit_solution(6821401912389380981)
XLA Ops:
  0.0 0.0 copy-start
  0.0 1.5 collective-permute-start
  1.5 3.1 %slice.9 = bf16[2,1024,512]{2,1,0:T(8,128)(2,1)} slice(bf16[3,1024,512]{2,1,0:T(8,128)(2,1)} %param.10), slice={[1:3], [0:1024], [0:512]} | slice | bytes 4194304 | tf_op jit(solution)/shard_map/slice | solution.py:147
  4.6 3.0 %copy.26 = bf16[2,1024,512]{1,2,0:T(8,128)(2,1)S(1)} copy(bf16[2,1024,512]{2,1,0:T(8,128)(2,1)} %slice.9) | data formatting | bytes 4194304
  7.5 1.6 copy.19
  9.1 0.0 copy-done
  9.1 0.8 constant_dynamic-slice_fusion
  10.0 15.2 %collective-permute-done = bf16[1024,512]{1,0:T(8,128)(2,1)} collective-permute-done((bf16[1024,512]{1,0:T(8,128)(2,1)}, bf16[1024,512]{1,0:T(8,128)(2,1)}, u32[]{:S(2)}, u32[]{:S(2)}) %collective-permute-start) | collective-permute-done | bytes 1048608 | tf_op jit(solution)/shard_map/ppermute | solution.py:108
  25.2 3.0 %maximum_select_fusion = bf16[1024,1024]{1,0:T(8,128)(2,1)S(1)} fusion(bf16[1024,512]{1,0:T(8,128)(2,1)} %collective-permute-done, bf16[1024,512]{1,0:T(8,128)(2,1)} %param.7, pred[]{:T(512)S(6)} %eq.3), kind=kLoop, calls=%fused_computation.10 | loop fusion | flops 9437184 | bytes 4194305 | tf_op jit(solution)/shard_map/jit(_where)/select_n | solution.py:109
  28.3 0.0 copy-start.7
  28.3 0.3 convert_reduce_fusion
  28.6 0.7 fusion.2
  29.3 0.0 copy-done.7
  29.3 0.0 copy-start.3
  29.4 3.7 %convolution_convert_fusion = bf16[1024,512]{1,0:T(8,128)(2,1)} fusion(bf16[3,1024,512]{2,1,0:T(8,128)(2,1)} %param.10, bf16[1024,1024]{1,0:T(8,128)(2,1)S(1)} %maximum_select_fusion, f32[1024]{0:T(1024)S(1)} %copy-done.7, f32[1024]{0:T(1024)S(1)} %add_rsqrt_fusion, f32[1024]{0:T(1024)S(1)} %broadcast_multiply_fusion), kind=kOutput, calls=%fused_computation.13 | convolution fusion | flops 1079508992 | bytes 4206592 | tf_op jit(solution)/shard_map/dot_general | solution.py:152
  33.0 0.0 copy-done.3
  33.0 2.4 convert_bitcast_fusion
  35.5 0.6 copy.27
  36.1 0.4 copy.20
  36.5 2.3 copy.21
  38.7 2.6 reshape.94
  41.4 2.4 copy.22
  43.7 2.3 copy.23
  46.0 3.1 %pad_maximum_fusion = bf16[16,768,128]{2,1,0:T(8,128)(2,1)} fusion(bf16[16,256,128]{2,1,0:T(8,128)(2,1)} %copy.23, bf16[16,512,128]{2,1,0:T(8,128)(2,1)S(1)} %bitcast.42), kind=kLoop, calls=%fused_computation.9 | loop fusion | flops 6291456 | bytes 6291456 | tf_op jit(solution)/shard_map/concatenate | solution.py:154
  49.1 0.0 copy-start.4
  49.1 6.3 %all-to-all-start = ((bf16[16,768,128]{2,1,0:T(8,128)(2,1)}), bf16[16,768,128]{2,1,0:T(8,128)(2,1)}, u32[]{:S(2)}, u32[]{:S(2)}) async-start(bf16[16,768,128]{2,1,0:T(8,128)(2,1)} %pad_maximum_fusion), calls=%async_computation | async-start | bytes 6291456 | tf_op jit(solution)/shard_map/all_to_all | solution.py:157
  55.5 0.0 copy-done.4
  55.5 0.0 copy-start.1
  55.5 0.0 copy-start.8
  55.5 1.6 collective-permute-start.1
  57.0 12.5 %collective-permute-done.1 = bf16[512,512]{1,0:T(8,128)(2,1)S(1)} collective-permute-done((bf16[512,512]{1,0:T(8,128)(2,1)S(1)}, bf16[512,512]{1,0:T(8,128)(2,1)S(1)}, u32[]{:S(2)}, u32[]{:S(2)}) %collective-permute-start.1) | collective-permute-done | bytes 524320 | tf_op jit(solution)/shard_map/ppermute | solution.py:120
  69.5 0.0 copy-start.5
  69.5 56.1 %all-to-all-done.got_ref = bf16[16,768,128]{2,1,0:T(8,128)(2,1)} async-done(((bf16[16,768,128]{2,1,0:T(8,128)(2,1)}), bf16[16,768,128]{2,1,0:T(8,128)(2,1)}, u32[]{:S(2)}, u32[]{:S(2)}) %all-to-all-start) | async-done | bytes 3145760 | tf_op jit(solution)/shard_map/all_to_all | solution.py:157
  125.7 0.0 copy-done.5
  125.7 3.1 %slice.11 = bf16[16,512,128]{2,1,0:T(8,128)(2,1)} slice(bf16[16,768,128]{2,1,0:T(8,128)(2,1)} %all-to-all-done.got_ref), slice={[0:16], [0:512], [0:128]} | slice | bytes 4194304 | tf_op jit(solution)/shard_map/slice | solution.py:163
  128.8 0.0 collective-permute-start.2
  128.8 0.0 copy-done.1
  128.8 0.2 reduce-window.8
  129.0 0.1 convert_reduce_fusion.1
  129.1 0.7 gather_fusion
  129.8 0.7 gather_fusion.1
  130.4 0.8 dynamic_slice.13
  131.2 0.0 copy-done.8
  131.2 0.6 dynamic_slice.12
  132.4 0.1 maximum_bitcast_fusion.g_ref
  132.5 0.7 collective-permute-done.2.rest_0_
  133.2 98.4 %shard_map.73 = bf16[16,256,128]{2,1,0:T(8,128)(2,1)S(1)} custom-call(s32[2,16]{1,0:T(2,128)S(1)} %pad_add_fusion.span, f32[1]{0:T(128)S(6)} %mul.31.c_ref, f32[1,128]{1,0:T(1,128)S(1)} %maximum_bitcast_fusion.g_ref, bf16[16,768,128]{2,1,0:T(8,128)(2,1)} %all-to-all-done.got_ref, bf16[16,512,128]{2,1,0:T(8,128)(2,1)S(1)} %collective-permute-done.2.rest_0_), custom_call_target="tpu_custom_call" | custom-call | flops 34359738368 | bytes 16777216 | tf_op jit(solution)/shard_map/pallas_call | solution.py:77
  231.6 29.6 %all_to_all.10 = bf16[16,256,128]{2,1,0:T(8,128)(2,1)S(1)} all-to-all(bf16[16,256,128]{2,1,0:T(8,128)(2,1)S(1)} %shard_map.73), channel_id=1, replica_groups=mesh['ctx'=16,'tp'=2] {'ctx'}, dimensions={0} | all-to-all | bytes 2097152 | tf_op jit(solution)/shard_map/all_to_all | solution.py:165
  261.2 0.5 copy.24
  261.7 2.0 copy.25
  263.8 1.8 reshape.97
  265.6 1.6 collective-permute-start.3
  267.1 0.0 copy-start.2
  267.1 0.0 copy-start.6
  267.1 0.7 fusion.7
  267.9 22.3 %collective-permute-done.3 = bf16[1024,512]{0,1:T(8,128)(2,1)S(1)} collective-permute-done((bf16[1024,512]{0,1:T(8,128)(2,1)S(1)}, bf16[1024,512]{0,1:T(8,128)(2,1)S(1)}, u32[]{:S(2)}, u32[]{:S(2)}) %collective-permute-start.3) | collective-permute-done | bytes 1048608 | tf_op jit(solution)/shard_map/ppermute | solution.py:170
  290.1 0.0 copy-done.2
  290.1 0.0 copy-done.6
  290.1 1.7 add_convert_fusion
  (6 shorter events, 0.0 us)
Async XLA Ops:
  0.0 9.1 %copy-start = (bf16[512,1024]{1,0:T(8,128)(2,1)S(1)}, bf16[512,1024]{1,0:T(8,128)(2,1)}, u32[]{:S(2)}) copy-start(bf16[512,1024]{1,0:T(8,128)(2,1)} %param.13) | copy-start | bytes 3145732
  0.0 25.2 %collective-permute-start = (bf16[1024,512]{1,0:T(8,128)(2,1)}, bf16[1024,512]{1,0:T(8,128)(2,1)}, u32[]{:S(2)}, u32[]{:S(2)}) collective-permute-start(bf16[1024,512]{1,0:T(8,128)(2,1)} %param.7), channel_id=1, source_target_pairs={{0,1},{1,0},{2,3},{3,2},{4,5},{5,4},{6,7},{7,6},{8,9},{9,8},{10,11... | collective-permute-start | bytes 3145736 | tf_op jit(solution)/shard_map/ppermute | solution.py:108
  28.3 1.1 copy-start.7
  29.3 3.7 %copy-start.3 = (bf16[1024,8,2,64]{0,3,2,1:T(8,128)(2,1)S(1)}, bf16[1024,8,2,64]{0,3,2,1:T(8,128)(2,1)}, u32[]{:S(2)}) copy-start(bf16[1024,8,2,64]{0,3,2,1:T(8,128)(2,1)} %copy.19) | copy-start | bytes 6291460
  49.1 6.3 %copy-start.4 = (bf16[512,512]{1,0:T(8,128)(2,1)S(1)}, bf16[512,512]{1,0:T(8,128)(2,1)}, u32[]{:S(2)}) copy-start(bf16[512,512]{1,0:T(8,128)(2,1)} %constant_dynamic-slice_fusion) | copy-start | bytes 1572868
  49.1 76.5 %all-to-all-start = ((bf16[16,768,128]{2,1,0:T(8,128)(2,1)}), bf16[16,768,128]{2,1,0:T(8,128)(2,1)}, u32[]{:S(2)}, u32[]{:S(2)}) async-start(bf16[16,768,128]{2,1,0:T(8,128)(2,1)} %pad_maximum_fusion), calls=%async_computation | async-start | bytes 6291456 | tf_op jit(solution)/shard_map/all_to_all | solution.py:157
  55.5 73.4 %copy-start.1 = (s32[4]{0:T(128)S(1)}, s32[4]{0:T(128)}, u32[]{:S(2)}) copy-start(s32[4]{0:T(128)} %param.8) | copy-start | bytes 52
  55.5 75.7 %copy-start.8 = (f32[8]{0:T(128)S(1)}, f32[8]{0:T(128)}, u32[]{:S(2)}) copy-start(f32[8]{0:T(128)} %param.11) | copy-start | bytes 100
  55.5 14.0 %collective-permute-start.1 = (bf16[512,512]{1,0:T(8,128)(2,1)S(1)}, bf16[512,512]{1,0:T(8,128)(2,1)S(1)}, u32[]{:S(2)}, u32[]{:S(2)}) collective-permute-start(bf16[512,512]{1,0:T(8,128)(2,1)S(1)} %copy-done.4), channel_id=1, source_target_pairs={{0,1},{1,0},{2,3},{3,2},{4,5},{5,4},{6,7},{7,6},{8,9},{9,8},{10,11... | collective-permute-start | bytes 1572872 | tf_op jit(solution)/shard_map/ppermute | solution.py:120
  69.5 56.2 %copy-start.5 = (bf16[512,512]{1,0:T(8,128)(2,1)}, bf16[512,512]{1,0:T(8,128)(2,1)S(1)}, u32[]{:S(2)}) copy-start(bf16[512,512]{1,0:T(8,128)(2,1)S(1)} %collective-permute-done.1) | copy-start | bytes 1572868
  128.8 4.4 %collective-permute-start.2 = (bf16[16,512,128]{2,1,0:T(8,128)(2,1)}, bf16[16,512,128]{2,1,0:T(8,128)(2,1)S(1)}, u32[]{:S(2)}, u32[]{:S(2)}) collective-permute-start(bf16[16,512,128]{2,1,0:T(8,128)(2,1)} %slice.11), channel_id=1, source_target_pairs={{0,2},{2,0},{4,6},{6,4},{8,10},{10,8},{12,14},{14,12},{16,18},{18,... | collective-permute-start | bytes 6291464 | tf_op jit(solution)/shard_map/ppermute | solution.py:163
  265.6 24.6 %collective-permute-start.3 = (bf16[1024,512]{0,1:T(8,128)(2,1)S(1)}, bf16[1024,512]{0,1:T(8,128)(2,1)S(1)}, u32[]{:S(2)}, u32[]{:S(2)}) collective-permute-start(bf16[1024,512]{0,1:T(8,128)(2,1)S(1)} %reshape.97), channel_id=1, source_target_pairs={{0,1},{1,0},{2,3},{3,2},{4,5},{5,4},{6,7},{7,6},{8,9},{9,8},{10,11... | collective-permute-start | bytes 3145736 | tf_op jit(solution)/shard_map/ppermute | solution.py:170
  267.1 23.0 %copy-start.2 = (bf16[1024,512]{1,0:T(8,128)(2,1)S(1)}, bf16[1024,512]{1,0:T(8,128)(2,1)}, u32[]{:S(2)}) copy-start(bf16[1024,512]{1,0:T(8,128)(2,1)} %param.7) | copy-start | bytes 3145732
  267.1 23.0 %copy-start.6 = (bf16[512,512]{1,0:T(8,128)(2,1)S(1)}, bf16[512,512]{1,0:T(8,128)(2,1)}, u32[]{:S(2)}) copy-start(bf16[512,512]{1,0:T(8,128)(2,1)} %copy-done.5) | copy-start | bytes 1572868
